TPU v7x, 32 devices: a whole 2x2x4 slice. The times are simulated.
32 devices in a mesh: grp: 2 (over y), seq: 8 (over z, x), head: 2 (over core).
Axes of the slice: x: 2, y: 2, z: 4, core: 2. Of those that a mesh axis runs over, the one named last changes fastest.
Arguments:
- queries: bfloat16 [8192, 1024], P(('grp', 'seq'), 'head'), parts along dimension 0, may hold values from -7 to 7
- keys: bfloat16 [8192, 1024], P(('grp', 'seq'), 'head'), parts along dimension 0, may hold values from -4 to 4
- values: bfloat16 [8192, 1024], P(('grp', 'seq'), 'head'), parts along dimension 0, may hold values from -6 to 6
- grad_out: bfloat16 [8192, 1024], P(('grp', 'seq'), 'head'), parts along dimension 0, may hold values from -6 to 6
- table_lengths: int32 [32], P('grp'), parts along dimension 0, may hold values from 1 to 32, 64 in all
- table_cols: int32 [32], P('grp'), parts along dimension 0, may hold values from 3 to 64
- caption_blocks: int32 [8], P('grp'), parts along dimension 0, may hold values from 0 to 63, as said below
- header_slots: int32 [128, 2], P(('grp', 'seq')), parts along dimension 0, may hold values from 0 to 3
Outputs:
- grad_queries: bfloat16 [8192, 1024], P(('grp', 'seq'), 'head'), parts along dimension 0
- grad_keys: bfloat16 [8192, 1024], P(('grp', 'seq'), 'head'), parts along dimension 0
- grad_values: bfloat16 [8192, 1024], P(('grp', 'seq'), 'head'), parts along dimension 0
There are 2 independent parts, one for each index of `grp`. A program takes and returns all parts, laid end to end along the dimension named above; each array names one. Nothing has to cross between parts.
Inputs may be any that keep to these rules, and one draw needn't show every extreme that they name: `caption_blocks`: 4 different block numbers, among them 0 and 63.
All inputs are finite; a program needn't handle non-finite values.
Results may differ from a plain program's by a relative error of at most 0.0095.
Values may be sent and summed in bfloat16 or wider, within the bound.
A program may use at most 64 MiB of HBM per device.

v0:
```python
import jax
import jax.numpy as jnp
from jax import lax
from jax.sharding import PartitionSpec as P

HEAD_DIM = 64
BLOCK = 64
RADIUS = 8


def extended(block, sides, width):
    for axis, dim in sides:
        count = lax.axis_size(axis)
        forward = [(i, i + 1) for i in range(count - 1)]
        backward = [(target, source) for source, target in forward]
        low = lax.ppermute(
            lax.slice_in_dim(block, block.shape[dim] - width, None, axis=dim), axis, forward
        )
        high = lax.ppermute(lax.slice_in_dim(block, 0, width, axis=dim), axis, backward)
        block = jnp.concatenate([low, block, high], axis=dim)
    return block


def from_behind(block, axis, distance):
    devices = range(lax.axis_size(axis))
    route = [(i - distance, i) for i in devices if i - distance in devices]
    return lax.ppermute(block, axis, route)


def cell_layout(cells, table_lengths, table_cols, total):
    lengths_cells = table_lengths * BLOCK
    starts = jnp.cumsum(lengths_cells, dtype=jnp.int32) - lengths_cells
    below = starts[None, :] <= cells[:, None]
    table_id = jnp.sum(below.astype(jnp.int32), axis=1, dtype=jnp.int32) - 1
    start_cell = jnp.max(jnp.where(below, starts[None, :], 0), axis=1)
    tables = jnp.arange(table_lengths.shape[0], dtype=jnp.int32)
    widths = jnp.sum(
        jnp.where(table_id[:, None] == tables[None, :], table_cols[None, :], 0),
        axis=1,
        dtype=jnp.int32,
    )
    column = (cells - start_cell) % jnp.maximum(widths, 1)
    inside = (cells >= 0) & (cells < total)
    return (table_id, cells - column, start_cell + column, inside)


def visibility(query_cells, key_cells, table_lengths, table_cols, total):
    query_table, query_row, query_col, query_inside = cell_layout(
        query_cells, table_lengths, table_cols, total
    )
    key_table, key_row, key_col, key_inside = cell_layout(
        key_cells, table_lengths, table_cols, total
    )
    near = jnp.abs(query_cells[:, None] // BLOCK - key_cells[None, :] // BLOCK) <= RADIUS
    shared = (query_row[:, None] == key_row[None, :]) | (query_col[:, None] == key_col[None, :])
    same_table = query_table[:, None] == key_table[None, :]
    return same_table & shared & near & query_inside[:, None] & key_inside[None, :]


def head_grads(query_head, grad_head, key_head, value_head, mask):
    scale = query_head.shape[1] ** (-0.5)
    scores = jnp.dot(query_head, key_head.T, preferred_element_type=jnp.float32) * scale
    scores = jnp.where(mask, scores, -1e30)
    top = jnp.max(scores, axis=1, keepdims=True)
    log_total = top + jnp.log(jnp.sum(jnp.exp(scores - top), axis=1, keepdims=True))
    probs = jnp.where(mask, jnp.exp(scores - log_total), 0.0)
    probs_low = probs.astype(jnp.bfloat16)
    outputs = jnp.dot(probs_low, value_head, preferred_element_type=jnp.float32)
    delta = jnp.sum(grad_head.astype(jnp.float32) * outputs, axis=1, keepdims=True)
    grad_probs = jnp.dot(grad_head, value_head.T, preferred_element_type=jnp.float32)
    grad_scores = (probs * (grad_probs - delta) * scale).astype(jnp.bfloat16)
    grad_query = jnp.dot(grad_scores, key_head, preferred_element_type=jnp.float32)
    grad_key = jnp.dot(grad_scores.T, query_head, preferred_element_type=jnp.float32)
    grad_value = jnp.dot(probs_low.T, grad_head, preferred_element_type=jnp.float32)
    return (grad_query, grad_key, grad_value, log_total[:, 0], delta[:, 0])


def shards(
    queries, keys, values, grad_out, table_lengths, table_cols, caption_blocks, header_slots
):
    rows = queries.shape[0]
    features = queries.shape[1]
    heads_here = features // HEAD_DIM
    blocks_here = rows // BLOCK
    reach = RADIUS * BLOCK
    span = rows + 2 * reach
    slots = caption_blocks.shape[0]
    total = jnp.sum(table_lengths, dtype=jnp.int32) * BLOCK
    device = lax.axis_index("seq")
    first_cell = device * rows
    own_cells = first_cell + jnp.arange(rows, dtype=jnp.int32)
    window_cells = first_cell - reach + jnp.arange(span, dtype=jnp.int32)

    def split_heads(matrix):
        return matrix.reshape(matrix.shape[0], heads_here, HEAD_DIM).transpose(1, 0, 2)

    def join_heads(stacked):
        return stacked.transpose(1, 0, 2).reshape(stacked.shape[1], features)

    pair = jnp.stack([keys, values])
    window_pair = extended(pair, (("seq", 1),), reach)
    owners = caption_blocks // blocks_here
    offsets = caption_blocks % blocks_here * BLOCK
    pieces = []
    for slot in range(slots):
        piece = lax.dynamic_slice_in_dim(pair, offsets[slot], BLOCK, 1)
        pieces.append(jnp.where(owners[slot] == device, piece.astype(jnp.float32), 0.0))
    caption_pair = lax.psum(jnp.concatenate(pieces, axis=1), "seq").astype(jnp.bfloat16)
    window_mask = visibility(own_cells, window_cells, table_lengths, table_cols, total)
    listed = jnp.any(
        header_slots[:, :, None] == jnp.arange(slots, dtype=jnp.int32)[None, None, :], axis=1
    )
    caption_mask = jnp.repeat(jnp.repeat(listed, BLOCK, axis=0), BLOCK, axis=1)
    full_mask = jnp.concatenate([window_mask, caption_mask], axis=1)
    key_all = jnp.concatenate([window_pair[0], caption_pair[0]], axis=0)
    value_all = jnp.concatenate([window_pair[1], caption_pair[1]], axis=0)

    def per_head(operands):
        query_head, grad_head, key_head, value_head = operands
        return head_grads(query_head, grad_head, key_head, value_head, full_mask)

    grad_query, grad_key, grad_value, log_totals, deltas = lax.map(
        per_head,
        (split_heads(queries), split_heads(grad_out), split_heads(key_all), split_heads(value_all)),
    )
    pair_grads = jnp.stack([join_heads(grad_key), join_heads(grad_value)])
    window_part = pair_grads[:, :span]
    caption_part = pair_grads[:, span:]
    from_next = from_behind(window_part[:, :reach], "seq", -1)
    from_prev = from_behind(window_part[:, reach + rows :].astype(jnp.bfloat16), "seq", 1).astype(
        jnp.float32
    )
    own = window_part[:, reach : reach + rows]
    own = own + from_next
    own = own + from_prev
    summed = lax.psum(caption_part, "seq")
    for slot in range(slots):
        current = lax.dynamic_slice_in_dim(own, offsets[slot], BLOCK, 1)
        addition = jnp.where(
            owners[slot] == device, summed[:, slot * BLOCK : (slot + 1) * BLOCK], 0.0
        )
        own = lax.dynamic_update_slice_in_dim(own, current + addition, offsets[slot], 1)
    return (
        join_heads(grad_query).astype(jnp.bfloat16),
        own[0].astype(jnp.bfloat16),
        own[1].astype(jnp.bfloat16),
    )


def solution(mesh):
    return jax.shard_map(
        shards,
        mesh=mesh,
        in_specs=(
            P(("grp", "seq"), "head"),
            P(("grp", "seq"), "head"),
            P(("grp", "seq"), "head"),
            P(("grp", "seq"), "head"),
            P("grp"),
            P("grp"),
            P("grp"),
            P(("grp", "seq"), None),
        ),
        out_specs=(P(("grp", "seq"), "head"), P(("grp", "seq"), "head"), P(("grp", "seq"), "head")),
        check_vma=False,
    )
```

profile of v0, /device:TPU:0, one launch (start us, length us, event | category | flops | bytes accessed | tf_op | source)
XLA Modules:
  0.0 362.2 jit_solution(18435362559625020508)
XLA Ops:
  10.8 5.8 %collective-permute-start = (bf16[2,512,512]{1,2,0:T(8,128)(2,1)}, bf16[2,512,512]{1,2,0:T(8,128)(2,1)}, u32[]{:S(2)}, u32[]{:S(2)}) collective-permute-start(bf16[2,512,512]{1,2,0:T(8,128)(2,1)} %pad_maximum_fusion.1), channel_id=1, source_target_pairs={{0,2},{2,4},{4,6},{6,8},{8,10},{10,12},{12,14},{1,3},{3,5},{5,7},{... | collective-permute-start | bytes 3145736 | tf_op jit(solution)/shard_map/ppermute | solution.py:16
  31.1 96.8 %all-reduce.4 = bf16[2,256,512]{1,2,0:T(8,128)(2,1)S(1)} all-reduce(f32[2,256,512]{1,2,0:T(8,128)S(1)} %pad_maximum_fusion.3), channel_id=1, replica_groups=mesh['grp'=2,'seq'=8,'head'=2] {'seq'}, use_global_device_ids=true, to_apply=%region_0.0 | all-reduce | flops 262144 | bytes 1572864 | tf_op jit(solution)/shard_map/psum | solution.py:108
  128.8 2.0 copy.39
  132.3 2.0 fusion.31
  134.4 1.7 pad_maximum_fusion
  136.3 1.4 maximum_bitcast_fusion.1
  137.9 87.8 %while.14 = (s32[]{:T(128)}, bf16[8,512,64]{1,2,0:T(8,128)(2,1)}, f32[8,1792,64]{1,2,0:T(8,128)}, f32[8,1792,64]{1,2,0:T(8,128)}, bf16[8,512,64]{1,2,0:T(8,128)(...) while((s32[]{:T(128)}, bf16[8,512,64]{1,2,0:T(8,128)(2,1)}, ...), condition=%wide.region_14.15_spmd, body=%wide.region_10.14_spmd.sunk | while | flops 720337920 | bytes 29847652 | solution.py:122
  139.4 2.6 fusion.105
  142.0 1.9 fusion.102
  143.9 2.4 multiply_convert_fusion.2
  150.4 2.6 fusion.105
  153.0 1.9 fusion.102
  154.9 2.4 multiply_convert_fusion.2
  161.4 2.6 fusion.105
  163.9 1.9 fusion.102
  165.9 2.4 multiply_convert_fusion.2
  169.5 1.3 fusion.103
  172.3 2.6 fusion.105
  174.9 1.9 fusion.102
  176.8 2.4 multiply_convert_fusion.2
  183.3 2.6 fusion.105
  185.9 1.9 fusion.102
  187.9 2.4 multiply_convert_fusion.2
  194.3 2.6 fusion.105
  196.9 1.9 fusion.102
  198.8 2.4 multiply_convert_fusion.2
  205.3 2.6 fusion.105
  207.8 1.9 fusion.102
  209.8 2.4 multiply_convert_fusion.2
  213.4 1.3 fusion.103
  216.2 2.6 fusion.105
  218.8 1.9 fusion.102
  220.7 2.4 multiply_convert_fusion.2
  224.3 1.3 fusion.103
  225.6 1.9 fusion.37
  228.8 2.4 fusion.33
  231.2 4.8 %collective-permute-start.3 = (bf16[2,512,512]{1,2,0:T(8,128)(2,1)}, bf16[2,512,512]{1,2,0:T(8,128)(2,1)S(1)}, u32[]{:S(2)}, u32[]{:S(2)}) collective-permute-start(bf16[2,512,512]{1,2,0:T(8,128)(2,1)} %fusion.33), channel_id=1, source_target_pairs={{0,2},{2,4},{4,6},{6,8},{8,10},{10,12},{12,14},{1,3},{3,5},{5,7},{... | collective-permute-start | bytes 3145736 | tf_op jit(solution)/shard_map/ppermute | solution.py:27
  236.0 2.1 pad_maximum_fusion.2
  238.1 2.0 copy.43
  240.2 52.9 %collective-permute-done.3 = bf16[2,512,512]{1,2,0:T(8,128)(2,1)S(1)} collective-permute-done((bf16[2,512,512]{1,2,0:T(8,128)(2,1)}, bf16[2,512,512]{1,2,0:T(8,128)(2,1)S(1)}, u32[]{:S(2)}, u32[]{:S(2)}) %collective-permute-start.3) | collective-permute-done | bytes 1048608 | tf_op jit(solution)/shard_map/ppermute | solution.py:27
  293.0 2.8 fusion.36
  295.8 33.5 %all-reduce.3.cloned.1.call-done = f32[2,256,512]{1,2,0:T(8,128)} async-done(((f32[2,256,512]{1,2,0:T(8,128)}), f32[2,256,512]{1,2,0:T(8,128)}) %all-reduce.3.cloned.1.call-update) | async-done | bytes 1048592 | tf_op jit(solution)/shard_map/psum | solution.py:136
  329.4 2.1 fusion.41
  331.5 4.6 %dynamic_update_slice.23 = f32[2,512,512]{1,2,0:T(8,128)S(1)} dynamic-update-slice(f32[2,512,512]{1,2,0:T(8,128)S(1)} %fusion.36, f32[2,64,512]{1,2,0:T(8,128)} %fusion.41, s32[]{:T(128)} %constant.101.clone.1, s32[]{:T(128)S(6)} %select_n.164, s32[]{:T(128)} %constant.101.clone.1) | dynamic-update-slice | bytes 524292 | tf_op jit(solution)/shard_map/dynamic_update_slice | solution.py:142
  336.1 2.2 fusion.40
  338.3 3.7 %dynamic_update_slice.24 = f32[2,512,512]{1,2,0:T(8,128)S(1)} dynamic-update-slice(f32[2,512,512]{1,2,0:T(8,128)S(1)} %dynamic_update_slice.23, f32[2,64,512]{1,2,0:T(8,128)} %fusion.40, s32[]{:T(128)} %constant.101.clone.1, s32[]{:T(128)S(6)} %select_n.167, s32[]{:T(128)} %constant.101.clone.1) | dynamic-update-slice | bytes 524292 | tf_op jit(solution)/shard_map/dynamic_update_slice | solution.py:142
  343.0 4.6 %dynamic_update_slice.25 = f32[2,512,512]{1,2,0:T(8,128)S(1)} dynamic-update-slice(f32[2,512,512]{1,2,0:T(8,128)S(1)} %dynamic_update_slice.24, f32[2,64,512]{1,2,0:T(8,128)} %fusion.39, s32[]{:T(128)} %constant.101.clone.1, s32[]{:T(128)S(6)} %select_n.170, s32[]{:T(128)} %constant.101.clone.1) | dynamic-update-slice | bytes 524292 | tf_op jit(solution)/shard_map/dynamic_update_slice | solution.py:142
  348.8 4.3 %dynamic_update_slice.26 = f32[2,512,512]{1,2,0:T(8,128)S(1)} dynamic-update-slice(f32[2,512,512]{1,2,0:T(8,128)S(1)} %dynamic_update_slice.25, f32[2,64,512]{1,2,0:T(8,128)} %fusion.38, s32[]{:T(128)} %constant.101.clone.1, s32[]{:T(128)S(6)} %select_n.173, s32[]{:T(128)} %constant.101.clone.1) | dynamic-update-slice | bytes 524292 | tf_op jit(solution)/shard_map/dynamic_update_slice | solution.py:142
  (99 shorter events, 44.6 us)
Async XLA Ops:
  7.2 10.8 %copy-start.5 = (s32[4]{0:T(128)S(1)}, s32[4]{0:T(128)}, u32[]{:S(2)}) copy-start(s32[4]{0:T(128)} %param.16) | copy-start | bytes 52
  7.2 16.3 %copy-start.3 = (s32[16]{0:T(128)S(1)}, s32[16]{0:T(128)}, u32[]{:S(2)}) copy-start(s32[16]{0:T(128)} %param.14) | copy-start | bytes 196
  7.2 322.2 %all-reduce.3.cloned.1.call-start = ((), (), s32[]{:S(2)}) async-start(), calls=%async_computation | async-start | bytes 2097152 | tf_op jit(solution)/shard_map/psum | solution.py:136
  10.8 123.6 %collective-permute-start = (bf16[2,512,512]{1,2,0:T(8,128)(2,1)}, bf16[2,512,512]{1,2,0:T(8,128)(2,1)}, u32[]{:S(2)}, u32[]{:S(2)}) collective-permute-start(bf16[2,512,512]{1,2,0:T(8,128)(2,1)} %pad_maximum_fusion.1), channel_id=1, source_target_pairs={{0,2},{2,4},{4,6},{6,8},{8,10},{10,12},{12,14},{1,3},{3,5},{5,7},{... | collective-permute-start | bytes 3145736 | tf_op jit(solution)/shard_map/ppermute | solution.py:16
  16.6 117.8 %collective-permute-start.1 = (bf16[2,512,512]{1,2,0:T(8,128)(2,1)}, bf16[2,512,512]{1,2,0:T(8,128)(2,1)}, u32[]{:S(2)}, u32[]{:S(2)}) collective-permute-start(bf16[2,512,512]{1,2,0:T(8,128)(2,1)} %pad_maximum_fusion.1), channel_id=1, source_target_pairs={{2,0},{4,2},{6,4},{8,6},{10,8},{12,10},{14,12},{3,1},{5,3},{7,5},{... | collective-permute-start | bytes 3145736 | tf_op jit(solution)/shard_map/ppermute | solution.py:19
  30.6 97.6 %copy-start.2 = (s32[16]{0:T(128)S(1)}, s32[16]{0:T(128)}, u32[]{:S(2)}) copy-start(s32[16]{0:T(128)} %param.15) | copy-start | bytes 196
  30.6 97.7 %copy-start.4 = (s32[8,2]{0,1:T(2,128)S(1)}, s32[8,2]{0,1:T(2,128)}, u32[]{:S(2)}) copy-start(s32[8,2]{0,1:T(2,128)} %param.17) | copy-start | bytes 196
  225.6 3.2 copy-start
  227.5 65.5 %collective-permute-start.2 = (f32[2,512,512]{1,2,0:T(8,128)S(1)}, f32[2,512,512]{1,2,0:T(8,128)}, u32[]{:S(2)}, u32[]{:S(2)}) collective-permute-start(f32[2,512,512]{1,2,0:T(8,128)S(1)} %fusion.37), channel_id=1, source_target_pairs={{2,0},{4,2},{6,4},{8,6},{10,8},{12,10},{14,12},{3,1},{5,3},{7,5},{... | collective-permute-start | bytes 6291464 | tf_op jit(solution)/shard_map/ppermute | solution.py:27
  231.2 61.8 %collective-permute-start.3 = (bf16[2,512,512]{1,2,0:T(8,128)(2,1)}, bf16[2,512,512]{1,2,0:T(8,128)(2,1)S(1)}, u32[]{:S(2)}, u32[]{:S(2)}) collective-permute-start(bf16[2,512,512]{1,2,0:T(8,128)(2,1)} %fusion.33), channel_id=1, source_target_pairs={{0,2},{2,4},{4,6},{6,8},{8,10},{10,12},{12,14},{1,3},{3,5},{5,7},{... | collective-permute-start | bytes 3145736 | tf_op jit(solution)/shard_map/ppermute | solution.py:27
  329.3 12.7 %copy-start.1 = (f32[2,256,512]{1,2,0:T(8,128)S(1)}, f32[2,256,512]{1,2,0:T(8,128)}, u32[]{:S(2)}) copy-start(f32[2,256,512]{1,2,0:T(8,128)} %all-reduce.3.cloned.1.call-done) | copy-start | bytes 3145732
Sparse Core Ops, SparseCore 0:
  238.2 91.0 all-reduce.2
where the time goes:
time: 364 us; the launch traced here: 362 us
  blocking collectives  96.8 us (27%)
  waiting for transfers between devices  86.4 us (24%)
  matrix products  82.4 us (23%)
  other arithmetic  29.8 us (8%)
  local copies, waits for them, and re-layouts  28.6 us (8%)
  between operations  24.9 us (7%)
  starting transfers between devices  13.2 us (4%)
    psum x1, blocking collectives, shards(): lax.psum(jnp.concatenate(pieces, axis=1), 'seq').astype(jnp.bfloat16)  96.8 us
    ppermute x2, waiting for transfers between devices, from_behind(): return lax.ppermute(block, axis, route)  52.9 us
    psum x1, waiting for transfers between devices, shards(): summed = lax.psum(caption_part, 'seq')  33.5 us
    dot_general x8, matrix products, head_grads(): jnp.dot(probs_low.T, grad_head, preferred_element_type=jnp.float32)  20.7 us
    dot_general x8, matrix products, head_grads(): jnp.dot(grad_head, value_head.T, preferred_element_type=jnp.float32)  19 us
    dynamic_update_slice x4, local copies, waits for them, and re-layouts, shards(): lax.dynamic_update_slice_in_dim(own, current + addition, offsets[slot], 1)  17.2 us
    dot_general x8, matrix products, head_grads(): outputs = jnp.dot(probs_low, value_head, preferred_element_type=jnp.float32)  15.3 us
    dot_general x8, matrix products, head_grads(): jnp.dot(grad_scores, key_head, preferred_element_type=jnp.float32)  10.4 us
  transfers between devices with their start and end apart: 5, of which 2 were waited for; matrix products, arithmetic and copies ran while one was open for 5% of the time, Pallas kernels for 0%

commit v1 on v0

v1 whole, which is shorter than its diff:
```python
import functools

import jax
import jax.numpy as jnp
from jax import lax
from jax.experimental import pallas as pl
from jax.experimental.pallas import tpu as pltpu
from jax.sharding import PartitionSpec as P

HEAD_DIM = 64
BLOCK = 64
RADIUS = 8
LANES = 128
TILE = 256
HEADS_PER_PAIR = LANES // HEAD_DIM
NEG = -1e30
MESH = pl.DeviceIdType.MESH


def cell_ids(cells, lengths_ref, cols_ref, total):
    def step(table, carry):
        start, here, width = carry
        inside = cells >= start
        here = jnp.where(inside, start, here)
        width = jnp.where(inside, cols_ref[table], width)
        return (start + lengths_ref[table] * BLOCK, here, width)

    _, here, width = lax.fori_loop(
        0, lengths_ref.shape[0], step, (jnp.int32(0), jnp.zeros_like(cells), jnp.ones_like(cells))
    )
    offset = cells - here
    widthf = width.astype(jnp.float32)
    lines = jnp.floor((offset.astype(jnp.float32) + 0.5) / widthf).astype(jnp.int32)
    column = offset - lines * width
    inside = (cells >= 0) & (cells < total)
    return (
        jnp.where(inside, cells - column, -1),
        jnp.where(inside, here + column, -1),
    )


def kernel(
    n, lengths_ref, cols_ref, caps_ref, header_ref, q_ref, k_ref, v_ref, g_ref,
    dq_ref, dk_ref, dv_ref,
    win, acc, bias, kt, sbuf, dpbuf, plow, dsc, qs,
    far_out, far_in, near_out, near_in, piece, rs_in, full, gpiece, grs_in, gfull,
    a_send, a_recv, b_send, b_recv, c_send, c_recv, d_send, d_recv,
    e_send, e_recv, f_send, f_recv, x_send, x_recv, y_send, y_recv,
):
    rows, features = q_ref.shape
    pairs = features // LANES
    tiles = rows // TILE
    reach = RADIUS * BLOCK
    span = rows + 2 * reach
    wchunks = (TILE + 2 * reach) // TILE
    slots = caps_ref.shape[0]
    cap_rows = slots * BLOCK
    nchunk = wchunks + cap_rows // TILE
    reducers = 2 * slots
    me = lax.axis_index("seq")
    odd = me % 2
    partner = me + 1 - 2 * odd
    ahead = lax.rem(me + 2, n)
    behind = lax.rem(me + n - 2, n)
    high = reach + rows
    near_at = pl.multiple_of((1 - odd) * high, TILE)
    far_at = pl.multiple_of(odd * high, TILE)
    forward_to = jnp.where(odd == 1, behind, ahead)
    back_to = jnp.where(odd == 1, ahead, behind)
    kv = (k_ref, v_ref)

    def peers(body):
        def step(j, carry):
            body(j, lax.rem(me + j, n), lax.rem(me + n - j, n))
            return carry

        lax.fori_loop(1, n, step, 0)

    def guarded(index, body):
        if n == reducers:
            body()
        else:
            pl.when(index < reducers)(body)

    barrier = pltpu.get_barrier_semaphore()
    peers(lambda j, to, source: pl.semaphore_signal(
        barrier, inc=1, device_id={"seq": to}, device_id_type=MESH))
    pl.semaphore_wait(barrier, n - 1)

    def remote(src, dst, send, recv, to):
        return pltpu.make_async_remote_copy(
            src_ref=src, dst_ref=dst, send_sem=send, recv_sem=recv,
            device_id={"seq": to}, device_id_type=MESH)

    def lanes(p):
        return pl.ds(pl.multiple_of(p * LANES, LANES), LANES)

    def copy_a(c, p):
        return remote(kv[c].at[:, lanes(p)], win.at[c, p, pl.ds(far_at, rows)],
                      a_send.at[c, p], a_recv.at[c, p], partner)

    def copy_b(c, p):
        return remote(win.at[c, p, pl.ds(near_at, rows)], win.at[c, p, pl.ds(far_at, rows)],
                      b_send.at[c, p], b_recv.at[c, p], forward_to)

    def copy_c(c, p):
        return remote(far_out.at[c, p], far_in.at[c, p], c_send.at[c, p], c_recv.at[c, p], back_to)

    def copy_d(c, p):
        return remote(near_out.at[c, p], near_in.at[c, p], d_send.at[c, p], d_recv.at[c, p], partner)

    def scatter(source_buf, dest, send, recv, j, to):
        return remote(source_buf.at[to], dest.at[me], send.at[j], recv.at[j], to)

    def gather(buf, send, recv, j, to):
        return remote(buf.at[me], buf.at[me], send.at[j], recv.at[j], to)

    def start_scatter(source_buf, dest, send, recv):
        peers(lambda j, to, source: guarded(
            to, lambda: scatter(source_buf, dest, send, recv, j, to).start()))

    def reduce_and_gather(source_buf, dest, out, send, recv, gsend, grecv):
        def mine():
            peers(lambda j, to, source: scatter(source_buf, dest, send, recv, j, to).wait_recv())
            total = source_buf[me].astype(jnp.float32)

            def add(j, value):
                return value + dest[lax.rem(me + j, n)].astype(jnp.float32)

            out[me] = lax.fori_loop(1, n, add, total).astype(jnp.bfloat16)
            peers(lambda j, to, source: gather(out, gsend, grecv, j, to).start())

        guarded(me, mine)

    def wait_gather(source_buf, dest, out, send, recv, gsend, grecv):
        peers(lambda j, to, source: guarded(
            source, lambda: gather(out, gsend, grecv, j, to).wait_recv()))
        guarded(me, lambda: peers(
            lambda j, to, source: gather(out, gsend, grecv, j, to).wait_send()))
        peers(lambda j, to, source: guarded(
            to, lambda: scatter(source_buf, dest, send, recv, j, to).wait_send()))

    blocks_here = rows // BLOCK
    for s in range(slots):
        owned = [
            jnp.where(caps_ref[s] == me * blocks_here + b, 1.0, 0.0).astype(jnp.bfloat16)
            for b in range(blocks_here)
        ]
        for c in range(2):
            offer = kv[c][:BLOCK] * owned[0]
            for b in range(1, blocks_here):
                offer = offer + kv[c][b * BLOCK:(b + 1) * BLOCK] * owned[b]
            piece[c * slots + s] = offer
    start_scatter(piece, rs_in, e_send, e_recv)
    for p in range(pairs):
        for c in range(2):
            copy_a(c, p).start()

    for p in range(pairs):
        for c in range(2):
            win[c, p, pl.ds(reach, rows)] = kv[c][:, p * LANES:(p + 1) * LANES]

    total_cells = lax.fori_loop(
        0, lengths_ref.shape[0], lambda t, value: value + lengths_ref[t] * BLOCK, jnp.int32(0))
    first = me * rows
    query_ids = []
    for t in range(tiles):
        cells = first + t * TILE + lax.broadcasted_iota(jnp.int32, (8, TILE), 1)
        row, col = cell_ids(cells, lengths_ref, cols_ref, total_cells)
        query_ids.append((row[:1], col[:1], cells[:1] // BLOCK))

    for chunk in range(span // TILE):
        cells = first - reach + chunk * TILE + lax.broadcasted_iota(jnp.int32, (TILE, LANES), 0)
        row, col = cell_ids(cells, lengths_ref, cols_ref, total_cells)
        key_block = (cells + reach) // BLOCK - RADIUS
        row, col, key_block = (
            jnp.concatenate([x] * (TILE // LANES), axis=1) for x in (row, col, key_block))
        for t in range(tiles):
            if 0 <= chunk - t < wchunks:
                qrow, qcol, qblock = query_ids[t]
                near = jnp.abs(key_block - qblock) <= RADIUS
                seen = near & ((row == qrow) | (col == qcol))
                bias[t, (chunk - t) * TILE:(chunk - t + 1) * TILE] = jnp.where(seen, 0.0, NEG)
    for t in range(tiles):
        local = (t * TILE + lax.broadcasted_iota(jnp.int32, (1, TILE), 1)) // BLOCK
        for s in range(slots):
            line = jnp.full((1, TILE), NEG, jnp.float32)
            for b in range(t * TILE // BLOCK, (t + 1) * TILE // BLOCK):
                hit = header_ref[b, 0] == s
                for extra in range(1, header_ref.shape[1]):
                    hit = hit | (header_ref[b, extra] == s)
                line = jnp.where(local == b, jnp.where(hit, 0.0, NEG), line)
            at = wchunks * TILE + s * BLOCK
            bias[t, at:at + BLOCK] = jnp.broadcast_to(line, (BLOCK, TILE))

    reduce_and_gather(piece, rs_in, full, e_send, e_recv, f_send, f_recv)
    for c in range(2):
        copy_a(c, 0).wait_recv()
        copy_b(c, 0).start()
    wait_gather(piece, rs_in, full, e_send, e_recv, f_send, f_recv)
    for p in range(pairs):
        for c in range(2):
            for s in range(slots):
                win[c, p, span + s * BLOCK:span + (s + 1) * BLOCK] = (
                    full[c * slots + s, :, p * LANES:(p + 1) * LANES])

    lane = lax.broadcasted_iota(jnp.int32, (TILE, LANES), 1) // HEAD_DIM

    def fold(x, op):
        return op(x.reshape(TILE // 8, 8, TILE), axis=0)

    def compute(p):
        acc[:, p] = jnp.zeros_like(acc[:, p])
        kt[...] = win[0, p].T

        def tile(t, carry):
            q_rows = pl.ds(pl.multiple_of(t * TILE, TILE), TILE)
            q = q_ref[q_rows, lanes(p)] * jnp.bfloat16(HEAD_DIM ** -0.5)
            g = g_ref[q_rows, lanes(p)]
            starts = [pl.multiple_of(t * TILE + i * TILE, TILE) for i in range(wchunks)]
            starts += [span + i * TILE for i in range(cap_rows // TILE)]
            zero = jnp.zeros_like(q)
            nt = (((1,), (1,)), ((), ()))
            grad_q = []
            for h in range(HEADS_PER_PAIR):
                qh = jnp.where(lane == h, q, zero)
                gh = jnp.where(lane == h, g, zero)
                qs[0, h * TILE:(h + 1) * TILE] = qh
                qs[1, h * TILE:(h + 1) * TILE] = gh
                top = jnp.full((8, TILE), NEG, jnp.float32)
                for i, at in enumerate(starts):
                    r = slice(i * TILE, (i + 1) * TILE)
                    scores = lax.dot_general(win[0, p, pl.ds(at, TILE)], qh, nt,
                                             preferred_element_type=jnp.float32) + bias[t, r]
                    sbuf[h, r] = scores
                    top = jnp.maximum(top, fold(scores, jnp.max))
                top = jnp.max(top, axis=0, keepdims=True)
                norm = jnp.zeros((8, TILE), jnp.float32)
                for i, at in enumerate(starts):
                    r = slice(i * TILE, (i + 1) * TILE)
                    e = jnp.exp(sbuf[h, r] - top)
                    sbuf[h, r] = e
                    norm = norm + fold(e, jnp.sum)
                inverse = 1.0 / jnp.sum(norm, axis=0, keepdims=True)
                delta = jnp.zeros((8, TILE), jnp.float32)
                for i, at in enumerate(starts):
                    r = slice(i * TILE, (i + 1) * TILE)
                    probs = sbuf[h, r] * inverse
                    sbuf[h, r] = probs
                    low = probs.astype(jnp.bfloat16)
                    plow[r, h * TILE:(h + 1) * TILE] = low
                    dp = lax.dot_general(win[1, p, pl.ds(at, TILE)], gh, nt,
                                         preferred_element_type=jnp.float32)
                    dpbuf[h, r] = dp
                    delta = delta + fold(low.astype(jnp.float32) * dp, jnp.sum)
                delta = jnp.sum(delta, axis=0, keepdims=True)
                gq = jnp.zeros((HEAD_DIM, TILE), jnp.float32)
                for i, at in enumerate(starts):
                    r = slice(i * TILE, (i + 1) * TILE)
                    ds = (sbuf[h, r] * (dpbuf[h, r] - delta)).astype(jnp.bfloat16)
                    dsc[r, h * TILE:(h + 1) * TILE] = ds
                    gq = gq + jnp.dot(kt[h * HEAD_DIM:(h + 1) * HEAD_DIM, pl.ds(at, TILE)], ds,
                                      preferred_element_type=jnp.float32)
                grad_q.append(gq)
            for i, at in enumerate(starts):
                r = slice(i * TILE, (i + 1) * TILE)
                acc[0, p, pl.ds(at, TILE)] += jnp.dot(
                    dsc[r], qs[0], preferred_element_type=jnp.float32)
                acc[1, p, pl.ds(at, TILE)] += jnp.dot(
                    plow[r], qs[1], preferred_element_type=jnp.float32)
            joined = jnp.concatenate(grad_q, axis=0) * (HEAD_DIM ** -0.5)
            dq_ref[q_rows, lanes(p)] = joined.T.astype(jnp.bfloat16)
            return carry

        lax.fori_loop(0, tiles, tile, 0)

    def combine(p):
        for c in range(2):
            copy_c(c, p).wait_recv()
            near_out[c, p] = (acc[c, p, pl.ds(near_at, rows)]
                              + far_in[c, p].astype(jnp.float32)).astype(jnp.bfloat16)
            copy_d(c, p).start()

    def pair(p, carry):
        @pl.when(p + 1 < pairs)
        def _():
            for c in range(2):
                copy_a(c, p + 1).wait_recv()
                copy_b(c, p + 1).start()

        for c in range(2):
            copy_b(c, p).wait_recv()
        compute(p)
        for c in range(2):
            far_out[c, p] = acc[c, p, pl.ds(far_at, rows)].astype(jnp.bfloat16)
            copy_c(c, p).start()
            for s in range(slots):
                gpiece[c * slots + s, :, lanes(p)] = acc[
                    c, p, span + s * BLOCK:span + (s + 1) * BLOCK].astype(jnp.bfloat16)

        @pl.when(p >= 1)
        def _():
            combine(p - 1)

        return carry

    lax.fori_loop(0, pairs, pair, 0)
    start_scatter(gpiece, grs_in, x_send, x_recv)
    combine(pairs - 1)
    reduce_and_gather(gpiece, grs_in, gfull, x_send, x_recv, y_send, y_recv)
    outs = (dk_ref, dv_ref)
    for p in range(pairs):
        for c in range(2):
            copy_d(c, p).wait_recv()
            acc[c, p, pl.ds(reach, rows)] += near_in[c, p].astype(jnp.float32)
    wait_gather(gpiece, grs_in, gfull, x_send, x_recv, y_send, y_recv)
    for b in range(blocks_here):
        weights = [jnp.where(caps_ref[s] == me * blocks_here + b, 1.0, 0.0) for s in range(slots)]
        r = slice(b * BLOCK, (b + 1) * BLOCK)
        for c in range(2):
            for p in range(pairs):
                ls = slice(p * LANES, (p + 1) * LANES)
                value = acc[c, p, reach + b * BLOCK:reach + (b + 1) * BLOCK]
                for s in range(slots):
                    value = value + gfull[c * slots + s, :, ls].astype(jnp.float32) * weights[s]
                outs[c][r, ls] = value.astype(jnp.bfloat16)
    for p in range(pairs):
        for c in range(2):
            copy_a(c, p).wait_send()
            copy_b(c, p).wait_send()
            copy_c(c, p).wait_send()
            copy_d(c, p).wait_send()


def shards(
    queries, keys, values, grad_out, table_lengths, table_cols, caption_blocks, header_slots
):
    n = lax.axis_size("seq")
    rows, features = queries.shape
    pairs = features // LANES
    tiles = rows // TILE
    slots = caption_blocks.shape[0]
    reducers = 2 * slots
    span = rows + 2 * RADIUS * BLOCK
    keys_all = span + slots * BLOCK
    seen_rows = TILE + 2 * RADIUS * BLOCK + slots * BLOCK
    bf16, f32 = jnp.bfloat16, jnp.float32
    vmem = pl.BlockSpec(memory_space=pltpu.VMEM)
    smem = pl.BlockSpec(memory_space=pltpu.SMEM)
    out = jax.ShapeDtypeStruct((rows, features), bf16)
    pair_sem = pltpu.SemaphoreType.DMA((2, pairs))
    peer_sem = pltpu.SemaphoreType.DMA((n,))
    halo = pltpu.VMEM((2, pairs, rows, LANES), bf16)
    chunks = pltpu.VMEM((reducers, BLOCK, features), bf16)
    arrivals = pltpu.VMEM((n, BLOCK, features), bf16)
    return pl.pallas_call(
        functools.partial(kernel, n),
        out_shape=(out, out, out),
        in_specs=[smem] * 4 + [vmem] * 4,
        out_specs=(vmem, vmem, vmem),
        scratch_shapes=[
            pltpu.VMEM((2, pairs, keys_all, LANES), bf16),
            pltpu.VMEM((2, pairs, keys_all, LANES), f32),
            pltpu.VMEM((tiles, seen_rows, TILE), f32),
            pltpu.VMEM((LANES, keys_all), bf16),
            pltpu.VMEM((HEADS_PER_PAIR, seen_rows, TILE), f32),
            pltpu.VMEM((HEADS_PER_PAIR, seen_rows, TILE), f32),
            pltpu.VMEM((seen_rows, HEADS_PER_PAIR * TILE), bf16),
            pltpu.VMEM((seen_rows, HEADS_PER_PAIR * TILE), bf16),
            pltpu.VMEM((2, HEADS_PER_PAIR * TILE, LANES), bf16),
            halo, halo, halo, halo,
            chunks, arrivals, chunks, chunks, arrivals, chunks,
        ] + [pair_sem] * 8 + [peer_sem] * 8,
        compiler_params=pltpu.CompilerParams(
            collective_id=0, has_side_effects=True, vmem_limit_bytes=56 * 2**20),
        cost_estimate=pl.CostEstimate(
            flops=10 * rows * seen_rows * features, transcendentals=rows * seen_rows * 8,
            bytes_accessed=14 * rows * features),
    )(table_lengths, table_cols, caption_blocks, header_slots, queries, keys, values, grad_out)


def solution(mesh):
    band = P(("grp", "seq"), "head")
    return jax.shard_map(
        shards,
        mesh=mesh,
        in_specs=(band, band, band, band, P("grp"), P("grp"), P("grp"), P(("grp", "seq"), None)),
        out_specs=(band, band, band),
        check_vma=False,
    )
```

time: 364 us -> 120 us (0.33)
  Pallas kernels: 0 us -> 114 us
  blocking collectives: 96.8 us -> 0 us
  waiting for transfers between devices: 86.4 us -> 0 us
  matrix products: 82.4 us -> 0 us
  other arithmetic: 29.8 us -> 0 us
  between operations: 24.9 us -> 0.65 us
  local copies, waits for them, and re-layouts: 28.6 us -> 5.3 us
  starting transfers between devices: 13.2 us -> 0 us
    pallas_call x0 -> x1, Pallas kernels: none -> 114 us  [shards(): pl.pallas_call(functools.partial(kernel, n), out_shape=(out, out, out), i...]
    psum x1 -> x0, blocking collectives: 96.8 us -> none  [shards(): lax.psum(jnp.concatenate(pieces, axis=1), 'seq').astype(jnp.bfloat16)]
    dot_general x48 -> x0, matrix products: 82.4 us -> none  [the longest x8 20.7 us: head_grads(): jnp.dot(probs_low.T, grad_head, preferred_element_type=jnp.float32)]
    ppermute x4 -> x0, waiting for transfers between devices: 52.9 us -> none  [the longest x2 52.9 us: from_behind(): return lax.ppermute(block, axis, route)]
    psum x1 -> x0, waiting for transfers between devices: 33.5 us -> none  [shards(): summed = lax.psum(caption_part, 'seq')]
    dynamic_update_slice x4 -> x0, local copies, waits for them, and re-layouts: 17.2 us -> none  [shards(): lax.dynamic_update_slice_in_dim(own, current + addition, offsets[slot], 1)]
    ppermute x4 -> x0, starting transfers between devices: 13.2 us -> none  [the longest x2 6.07 us: from_behind(): return lax.ppermute(block, axis, route)]
    add x14 -> x0, other arithmetic: 9.33 us -> none  [the longest x4 6.47 us: shards(): current + addition]
  transfers between devices with their start and end apart: 5 -> 0, of which waited for: 2 -> 0; matrix products, arithmetic and copies ran while one was open for 5% -> 0% of each run, Pallas kernels for 0% -> 0%
where the time goes in v1:
time: 120 us
  Pallas kernels  114 us (95%)
  local copies, waits for them, and re-layouts  5.3 us (4%)
    pallas_call x1, Pallas kernels, shards(): pl.pallas_call(functools.partial(kernel, n), out_shape=(out, out, out), i...  114 us
    unnamed x8, local copies, waits for them, and re-layouts  5.3 us

profile of v1, /device:TPU:0, one launch (start us, length us, event | category | flops | bytes accessed | tf_op | source)
XLA Modules:
  0.0 119.5 jit_solution(8268202703317973440)
XLA Ops:
  0.6 1.3 %copy.11.header_ref = s32[8,2]{1,0:T(8,128)} copy(s32[8,2]{0,1:T(2,128)} %param.15) | data formatting | bytes 128 | tf_op args[7]
  2.0 113.6 %shard_map.103 = (bf16[512,512]{1,0:T(8,128)(2,1)}, bf16[512,512]{1,0:T(8,128)(2,1)}, bf16[512,512]{1,0:T(8,128)(2,1)}) custom-call(s32[16]{0:T(128)} %lengths_ref.1, s32[16]{0:T(128)} %cols_ref.1, s32[4]{0:T(128)} %caps_ref.1, s32[8,2]{1,0:T(8,128)} %copy.11.header_ref, bf16[512,512]{1,0:T(8,128)(2,1)} %q_ref.1, bf16[512,512]{1,0:T(8,128)(2,1)} %k_ref.1, ...), custom_call_target="tpu_custom_call" | custom-call | flops 4026531840 | bytes 3670016 | tf_op jit(solution)/shard_map/pallas_call | solution.py:356
  115.6 0.0 copy-start.1
  115.6 1.9 %copy.15 = bf16[512,512]{1,0:T(8,128)(2,1)} copy(bf16[512,512]{1,0:T(8,128)(2,1)} %get-tuple-element.6) | data formatting | bytes 1048576
  117.5 0.0 copy-done.1
  117.5 0.0 copy-start
  117.5 0.8 copy.16
  118.3 0.4 copy-done
  118.7 0.8 copy.17
Async XLA Ops:
  115.6 1.9 %copy-start.1 = (bf16[512,512]{1,0:T(8,128)(2,1)S(1)}, bf16[512,512]{1,0:T(8,128)(2,1)}, u32[]{:S(2)}) copy-start(bf16[512,512]{1,0:T(8,128)(2,1)} %get-tuple-element.7) | copy-start | bytes 1572868
  117.5 1.2 %copy-start = (bf16[512,512]{1,0:T(8,128)(2,1)S(1)}, bf16[512,512]{1,0:T(8,128)(2,1)}, u32[]{:S(2)}) copy-start(bf16[512,512]{1,0:T(8,128)(2,1)} %get-tuple-element.8) | copy-start | bytes 1572868

commit v2 on v1

--- a/solution.py
+++ b/solution.py
@@ -152,9 +152,8 @@
                 offer = offer + kv[c][b * BLOCK:(b + 1) * BLOCK] * owned[b]
             piece[c * slots + s] = offer
     start_scatter(piece, rs_in, e_send, e_recv)
-    for p in range(pairs):
-        for c in range(2):
-            copy_a(c, p).start()
+    for c in range(2):
+        copy_a(c, 0).start()
 
     for p in range(pairs):
         for c in range(2):
@@ -169,6 +168,7 @@
         row, col = cell_ids(cells, lengths_ref, cols_ref, total_cells)
         query_ids.append((row[:1], col[:1], cells[:1] // BLOCK))
 
+    reduce_and_gather(piece, rs_in, full, e_send, e_recv, f_send, f_recv)
     for chunk in range(span // TILE):
         cells = first - reach + chunk * TILE + lax.broadcasted_iota(jnp.int32, (TILE, LANES), 0)
         row, col = cell_ids(cells, lengths_ref, cols_ref, total_cells)
@@ -193,11 +193,13 @@
             at = wchunks * TILE + s * BLOCK
             bias[t, at:at + BLOCK] = jnp.broadcast_to(line, (BLOCK, TILE))
 
-    reduce_and_gather(piece, rs_in, full, e_send, e_recv, f_send, f_recv)
     for c in range(2):
         copy_a(c, 0).wait_recv()
         copy_b(c, 0).start()
     wait_gather(piece, rs_in, full, e_send, e_recv, f_send, f_recv)
+    for p in range(1, pairs):
+        for c in range(2):
+            copy_a(c, p).start()
     for p in range(pairs):
         for c in range(2):
             for s in range(slots):

time: 120 us -> 127 us (1.058)
  Pallas kernels: 114 us -> 121 us
    pallas_call x1, Pallas kernels: 114 us -> 121 us  [shards(): pl.pallas_call(functools.partial(kernel, n), out_shape=(out, out, out), i...]
where the time goes in v2:
time: 127 us
  Pallas kernels  121 us (95%)
  local copies, waits for them, and re-layouts  5.3 us (4%)
    pallas_call x1, Pallas kernels, shards(): pl.pallas_call(functools.partial(kernel, n), out_shape=(out, out, out), i...  121 us
    unnamed x8, local copies, waits for them, and re-layouts  5.3 us

profile of v2, /device:TPU:0, one launch (start us, length us, event | category | flops | bytes accessed | tf_op | source)
XLA Modules:
  0.0 126.6 jit_solution(6956986538180569343)
XLA Ops:
  0.6 1.3 %copy.11.header_ref = s32[8,2]{1,0:T(8,128)} copy(s32[8,2]{0,1:T(2,128)} %param.15) | data formatting | bytes 128 | tf_op args[7]
  2.0 120.6 %shard_map.103 = (bf16[512,512]{1,0:T(8,128)(2,1)}, bf16[512,512]{1,0:T(8,128)(2,1)}, bf16[512,512]{1,0:T(8,128)(2,1)}) custom-call(s32[16]{0:T(128)} %lengths_ref.1, s32[16]{0:T(128)} %cols_ref.1, s32[4]{0:T(128)} %caps_ref.1, s32[8,2]{1,0:T(8,128)} %copy.11.header_ref, bf16[512,512]{1,0:T(8,128)(2,1)} %q_ref.1, bf16[512,512]{1,0:T(8,128)(2,1)} %k_ref.1, ...), custom_call_target="tpu_custom_call" | custom-call | flops 4026531840 | bytes 3670016 | tf_op jit(solution)/shard_map/pallas_call | solution.py:358
  122.6 0.0 copy-start.1
  122.6 1.9 %copy.15 = bf16[512,512]{1,0:T(8,128)(2,1)} copy(bf16[512,512]{1,0:T(8,128)(2,1)} %get-tuple-element.6) | data formatting | bytes 1048576
  124.6 0.0 copy-done.1
  124.6 0.0 copy-start
  124.6 0.8 copy.16
  125.4 0.4 copy-done
  125.8 0.8 copy.17
Async XLA Ops:
  122.6 1.9 %copy-start.1 = (bf16[512,512]{1,0:T(8,128)(2,1)S(1)}, bf16[512,512]{1,0:T(8,128)(2,1)}, u32[]{:S(2)}) copy-start(bf16[512,512]{1,0:T(8,128)(2,1)} %get-tuple-element.7) | copy-start | bytes 1572868
  124.6 1.2 copy-start
